TPU v7x, 256 devices: a whole 4x4x8 slice. The times are simulated.
256 devices in a mesh: date: 32 (over y, z_hi, core), tile: 8 (over z_lo, x).
Axes of the slice: x: 4, y: 4, z: 8 (z_hi: 4, z_lo: 2; z = z_hi * 2 + z_lo), core: 2. Of those that a mesh axis runs over, the one named last changes fastest.
Arguments:
- latest_model_output: float32 [2, 24, 16, 64, 128], P(None, None, None, 'tile', 'date'), may hold values from -6 to 6
- bygone_model_outputs: float32 [128, 24, 16, 64, 128], P('date', None, None, 'tile'), may hold values from -6 to 6
- sensor_reports: float32 [128, 24, 64, 128], P('date', None, 'tile'), may hold values from -6 to 6
- input_variable_scaling: float32 [16], replicated, may hold values from 0.25 to 4
- stepahead_blur_scale: float32 [24], replicated, may hold values from 0.02 to 0.08
- bygone_annual_ordinal: int32 [128], P('date'), may hold values from 0 to 364
- launch_annual_ordinal: int32 [2], replicated, may hold values from 0 to 364
Outputs:
- analog_mean: float32 [2, 24, 64, 128], P(None, None, 'tile', 'date')
All inputs are finite; a program needn't handle non-finite values.
Results may differ from a plain program's by a relative error of at most 0.0003.
Values sent between devices are 32-bit elements; how exact they have to be, the bound alone decides.
A program may use at most 128 MiB of HBM per device.

v0:
```python
import math

import jax
import jax.numpy as jnp
from jax import lax
from jax.sharding import PartitionSpec as P

WIN_HALF = 3


season_gain = 0.5


def extended(x, sides, width):
    for axis, dim in sides:
        size, length = (lax.axis_size(axis), x.shape[dim])
        up = [(i, (i + 1) % size) for i in range(size - 1)]
        down = [(j, i) for i, j in up]
        last = lax.slice_in_dim(x, length - width, length, axis=dim)
        initial = lax.slice_in_dim(x, 0, width, axis=dim)
        before = lax.ppermute(last, axis, up)
        after = lax.ppermute(initial, axis, down)
        x = jnp.concatenate([before, x, after], axis=dim)
    return x


def season_term(calendar, today):
    return season_gain * (
        1.0 - jnp.cos(2.0 * math.pi * (calendar - today).astype(jnp.float32) / 365.0)
    )


def lead_window(diffsq, reach):
    lead_count = diffsq.shape[1]
    padded = jnp.pad(diffsq, ((0, 0), (reach, reach), (0, 0), (0, 0)))
    lead_total = padded[:, 0:lead_count]
    for offset in range(1, 2 * reach + 1):
        lead_total = lead_total + padded[:, offset : offset + lead_count]
    return lead_total


def space_window(lead_total, row_count, col_count):
    padded = jnp.pad(lead_total, [(0, 0)] * (lead_total.ndim - 1) + [(1, 1)])
    row_total = (
        padded[..., 0:row_count, :]
        + padded[..., 1 : row_count + 1, :]
        + padded[..., 2 : row_count + 2, :]
    )
    return (
        row_total[..., 0:col_count]
        + row_total[..., 1 : col_count + 1]
        + row_total[..., 2 : col_count + 2]
    )


def cycle_distance(current, bygone_sample, input_variable_scaling, calendar, today, reach):
    row_count = bygone_sample.shape[3] - 2
    col_count = bygone_sample.shape[4]
    feature_discrepancy = current[None] - bygone_sample
    diffsq = (
        jnp.sum(
            feature_discrepancy
            * feature_discrepancy
            * input_variable_scaling[None, None, :, None, None],
            axis=2,
        )
        / bygone_sample.shape[2]
    )
    totals = space_window(lead_window(diffsq, reach), row_count, col_count)
    return totals / (9.0 * (2 * reach + 1)) + season_term(calendar, today)[:, None, None, None]


def local(
    latest_model_output,
    bygone_model_outputs,
    sensor_reports,
    input_variable_scaling,
    stepahead_blur_scale,
    bygone_annual_ordinal,
    launch_annual_ordinal,
):
    gathered_amounts = lax.all_gather(latest_model_output, "date", axis=4, tiled=True)
    current = extended(gathered_amounts, (("tile", 3),), 1)
    bygone_sample = extended(bygone_model_outputs, (("tile", 3),), 1)
    per_cycle = []
    for cycle_index in range(current.shape[0]):
        per_cycle.append(
            cycle_distance(
                current[cycle_index],
                bygone_sample,
                input_variable_scaling,
                bygone_annual_ordinal,
                launch_annual_ordinal[cycle_index],
                WIN_HALF,
            )
        )
    analog_metric = jnp.stack(per_cycle, axis=0)
    local_min = jnp.min(analog_metric, axis=1)
    spread_five = stepahead_blur_scale[None, None, :, None, None]
    nearest = lax.pmin(local_min, "date")
    kernel = jnp.exp(-(analog_metric - nearest[:, None]) / spread_five)
    numer = jnp.sum(kernel * sensor_reports[None], axis=1)
    denom = jnp.sum(kernel, axis=1)
    numer, denom = (
        lax.psum_scatter(numer, "date", scatter_dimension=3, tiled=True),
        lax.psum_scatter(denom, "date", scatter_dimension=3, tiled=True),
    )
    return numer / denom


def solution(mesh):
    placed = (
        P(None, None, None, "tile", "date"),
        P("date", None, None, "tile", None),
        P("date", None, "tile", None),
        P(),
        P(),
        P("date"),
        P(),
    )
    return jax.shard_map(
        local, mesh=mesh, in_specs=placed, out_specs=P(None, None, "tile", "date"), check_vma=False
    )
```

profile of v0, /device:TPU:7, one launch (start us, length us, event | category | flops | bytes accessed | tf_op | source)
XLA Modules:
  0.0 658.6 jit_solution(12294619305230223706)
XLA Ops:
  6.5 0.0 all-gather.2.cloned.1.call-start
  6.5 1.9 copy.21
  8.4 0.0 all-gather.2.cloned.1.call-update
  8.5 0.0 all-reduce.6.cloned.1.call-start
  8.5 109.6 %all-gather.2.cloned.1.call-done = f32[2,24,16,8,128]{1,3,2,0,4:T(8,128)} async-done(((f32[2,24,16,8,4]{1,3,2,0,4:T(8,128)}), f32[2,24,16,8,128]{1,3,2,0,4:T(8,128)}) %all-gather.2.cloned.1.call-update) | async-done | bytes 3145744 | tf_op jit(solution)/shard_map/all_gather | solution.py:82
  118.1 15.2 %fusion.24 = (f32[2,24,16,1,128]{1,3,2,0,4:T(1,128)}, f32[2,24,16,1,128]{1,3,2,0,4:T(1,128)S(1)}) fusion(f32[2,24,16,8,128]{1,3,2,0,4:T(8,128)} %all-gather.2.cloned.1.call-done), kind=kLoop, calls=%fused_computation.59 | loop fusion | bytes 1572864 | tf_op jit(solution)/shard_map/slice | solution.py:19
  133.2 0.0 copy-start.1
  133.2 0.0 copy-start.3
  133.2 2.8 copy.22
  136.0 15.9 %collective-permute-start = (f32[2,24,16,1,128]{4,2,3,1,0:T(8,128)S(1)}, f32[2,24,16,1,128]{4,2,3,1,0:T(8,128)}, u32[]{:S(2)}, u32[]{:S(2)}) collective-permute-start(f32[2,24,16,1,128]{4,2,3,1,0:T(8,128)S(1)} %copy.22), channel_id=1, source_target_pairs={{0,1},{1,2},{2,3},{3,4},{4,5},{5,6},{6,7},{8,9},{9,10},{10,11},{11... | collective-permute-start | bytes 1179656 | tf_op jit(solution)/shard_map/ppermute | solution.py:21
  151.9 2.1 copy.23
  153.9 1.9 collective-permute-start.1
  155.9 7.5 %fusion.25 = (f32[4,24,16,1,128]{4,3,2,1,0:T(1,128)}, f32[4,24,16,1,128]{4,3,2,1,0:T(1,128)}) fusion(f32[4,24,16,8,128]{4,3,2,1,0:T(8,128)} %param.8), kind=kLoop, calls=%fused_computation.60 | loop fusion | bytes 3145728 | tf_op jit(solution)/shard_map/slice | solution.py:19
  163.3 5.5 collective-permute-start.2
  168.8 2.1 collective-permute-start.3
  170.9 0.0 copy-done.1
  170.9 0.6 fusion.26
  171.5 0.0 copy-done.3
  171.5 1.3 subtract_multiply_fusion.1
  172.9 11.7 %copy.24 = f32[2,24,16,8,128]{4,2,3,1,0:T(8,128)S(1)} copy(f32[2,24,16,8,128]{1,3,2,0,4:T(8,128)} %all-gather.2.cloned.1.call-done) | data formatting | bytes 6291456 | tf_op jit(solution)/shard_map/all_gather | solution.py:82
  184.6 0.0 collective-permute-done
  184.6 0.0 collective-permute-done.1
  184.6 1.5 pad_maximum_fusion.1
  186.1 0.0 slice-start
  186.1 0.3 slice_bitcast_fusion
  186.4 0.0 slice-start.1
  186.4 0.0 copy-start.2
  186.4 0.8 copy.25
  187.2 0.8 copy.30
  188.0 0.0 collective-permute-done.2
  188.0 3.0 collective-permute-done.3
  191.1 0.0 slice-done
  191.1 0.0 slice-done.1
  191.1 0.0 copy-done.2
  191.1 8.0 %multiply_reduce_fusion.1 = (f32[4,24,10,128]{3,2,1,0:T(8,128)S(1)}, f32[4,24,10,128]{3,2,1,0:T(8,128)S(1)}) fusion(f32[4,24,16,1,128]{4,3,2,1,0:T(1,128)} %bitcast.2, f32[4,24,16,8,128]{4,3,2,1,0:T(8,128)S(1)} %bitcast.15, f32[4,24,16,1,128]{4,3,2,1,0:T(1,128)} %bitcast.1, f32[16]{0:T(128)S(1)} %copy-done.2, f32[24,16,10,128]{3,2,1,0:T(8,128)S(1)} %copy.25, ...), kind=kLoop, calls=%fused_computation.2 | loop fusion | flops 19415040 | bytes 12779584 | tf_op jit(solution)/shard_map/reduce_sum | solution.py:61
  199.1 0.1 broadcast_multiply_fusion
  199.2 0.2 fusion.5
  199.4 0.7 fusion.13
  200.1 0.0 copy-start
  200.1 0.0 copy-start.4
  200.1 0.2 fusion.11
  200.3 0.7 fusion.15
  201.0 0.3 fusion.22
  201.2 0.3 fusion.19
  201.5 0.7 fusion.16
  202.2 0.0 all-reduce.6.cloned.1.call-update
  202.2 0.0 reduce-scatter.3.cloned.1.call-start
  202.3 269.2 %all-reduce.6.cloned.1.call-done = f32[2,24,8,128]{3,2,1,0:T(8,128)} async-done(((f32[2,24,8,128]{3,2,1,0:T(8,128)}), f32[2,24,8,128]{3,2,1,0:T(8,128)}) %all-reduce.6.cloned.1.call-update) | async-done | bytes 196624 | tf_op jit(solution)/shard_map/pmin | solution.py:100
  471.5 0.0 copy-done
  471.5 0.0 copy-done.4
  471.5 1.2 fusion.23
  472.7 1.4 copy.31
  474.1 0.0 reduce-scatter.3.cloned.1.call-update
  474.1 0.0 reduce-scatter.5.cloned.1.call-start
  474.2 1.4 copy.32
  475.6 0.0 reduce-scatter.5.cloned.1.call-update
  475.6 84.8 %reduce-scatter.3.cloned.1.call-done = f32[2,24,8,4]{1,2,0,3:T(8,128)} async-done(((f32[2,24,8,128]{1,2,0,3:T(8,128)}), f32[2,24,8,4]{1,2,0,3:T(8,128)}) %reduce-scatter.3.cloned.1.call-update) | async-done | bytes 6160 | tf_op jit(solution)/shard_map/reduce_scatter | solution.py:105
  560.4 90.3 %reduce-scatter.5.cloned.1.call-done = f32[2,24,8,4]{1,2,0,3:T(8,128)} async-done(((f32[2,24,8,128]{1,2,0,3:T(8,128)}), f32[2,24,8,4]{1,2,0,3:T(8,128)}) %reduce-scatter.5.cloned.1.call-update) | async-done | bytes 6160 | tf_op jit(solution)/shard_map/reduce_scatter | solution.py:106
  650.6 0.8 div.40
  651.4 0.6 copy.33
  (1 shorter events, 0.0 us)
Async XLA Ops:
  6.5 111.5 %all-gather.2.cloned.1.call-start = ((), (), s32[]{:S(2)}) async-start(), calls=%async_computation.2 | async-start | bytes 17301504 | tf_op jit(solution)/shard_map/all_gather | solution.py:82
  8.5 463.0 %all-reduce.6.cloned.1.call-start = ((), (), s32[]{:S(2)}) async-start(), calls=%async_computation.3 | async-start | bytes 393216 | tf_op jit(solution)/shard_map/pmin | solution.py:100
  133.2 37.7 %copy-start.1 = (s32[2]{0:T(128)S(1)}, s32[2]{0:T(128)}, u32[]{:S(2)}) copy-start(s32[2]{0:T(128)} %param.13) | copy-start | bytes 28
  133.2 38.3 %copy-start.3 = (s32[4]{0:T(128)S(1)}, s32[4]{0:T(128)}, u32[]{:S(2)}) copy-start(s32[4]{0:T(128)} %param.12) | copy-start | bytes 52
  136.0 48.5 %collective-permute-start = (f32[2,24,16,1,128]{4,2,3,1,0:T(8,128)S(1)}, f32[2,24,16,1,128]{4,2,3,1,0:T(8,128)}, u32[]{:S(2)}, u32[]{:S(2)}) collective-permute-start(f32[2,24,16,1,128]{4,2,3,1,0:T(8,128)S(1)} %copy.22), channel_id=1, source_target_pairs={{0,1},{1,2},{2,3},{3,4},{4,5},{5,6},{6,7},{8,9},{9,10},{10,11},{11... | collective-permute-start | bytes 1179656 | tf_op jit(solution)/shard_map/ppermute | solution.py:21
  153.9 30.6 %collective-permute-start.1 = (f32[2,24,16,1,128]{4,2,3,1,0:T(8,128)}, f32[2,24,16,1,128]{4,2,3,1,0:T(8,128)}, u32[]{:S(2)}, u32[]{:S(2)}) collective-permute-start(f32[2,24,16,1,128]{4,2,3,1,0:T(8,128)} %copy.23), channel_id=1, source_target_pairs={{1,0},{2,1},{3,2},{4,3},{5,4},{6,5},{7,6},{9,8},{10,9},{11,10},{12... | collective-permute-start | bytes 1179656 | tf_op jit(solution)/shard_map/ppermute | solution.py:22
  163.3 24.7 %collective-permute-start.2 = (f32[4,24,16,1,128]{4,2,3,1,0:T(8,128)}, f32[4,24,16,1,128]{4,2,3,1,0:T(8,128)}, u32[]{:S(2)}, u32[]{:S(2)}) collective-permute-start(f32[4,24,16,1,128]{4,2,3,1,0:T(8,128)} %bitcast.8), channel_id=1, source_target_pairs={{0,1},{1,2},{2,3},{3,4},{4,5},{5,6},{6,7},{8,9},{9,10},{10,11},{11... | collective-permute-start | bytes 2359304 | tf_op jit(solution)/shard_map/ppermute | solution.py:21
  168.8 22.3 %collective-permute-start.3 = (f32[4,24,16,1,128]{4,2,3,1,0:T(8,128)}, f32[4,24,16,1,128]{4,2,3,1,0:T(8,128)}, u32[]{:S(2)}, u32[]{:S(2)}) collective-permute-start(f32[4,24,16,1,128]{4,2,3,1,0:T(8,128)} %bitcast.9), channel_id=1, source_target_pairs={{1,0},{2,1},{3,2},{4,3},{5,4},{6,5},{7,6},{9,8},{10,9},{11,10},{12... | collective-permute-start | bytes 2359304 | tf_op jit(solution)/shard_map/ppermute | solution.py:22
  186.1 5.0 slice-start
  186.4 4.7 slice-start.1
  186.4 4.7 copy-start.2
  200.1 271.4 %copy-start = (f32[4,24,8,128]{3,2,1,0:T(8,128)S(1)}, f32[4,24,8,128]{3,2,1,0:T(8,128)}, u32[]{:S(2)}) copy-start(f32[4,24,8,128]{3,2,1,0:T(8,128)} %param.9) | copy-start | bytes 1179652
  200.1 271.4 %copy-start.4 = (f32[24]{0:T(128)S(1)}, f32[24]{0:T(128)}, u32[]{:S(2)}) copy-start(f32[24]{0:T(128)} %param.11) | copy-start | bytes 292
  202.2 358.1 %reduce-scatter.3.cloned.1.call-start = ((), (), s32[]{:S(2)}) async-start(), calls=%async_computation.4 | async-start | bytes 1081344 | tf_op jit(solution)/shard_map/reduce_scatter | solution.py:105
  474.1 176.5 %reduce-scatter.5.cloned.1.call-start = ((), (), s32[]{:S(2)}) async-start(), calls=%async_computation.5 | async-start | bytes 1081344 | tf_op jit(solution)/shard_map/reduce_scatter | solution.py:106
Sparse Core Ops, SparseCore 0:
  9.9 108.1 all-gather.1
  202.4 269.0 all-reduce.5
  475.7 84.5 reduce-scatter.2
  564.0 86.5 reduce-scatter.4
where the time goes:
time: 661 us; the launch traced here: 659 us
  waiting for transfers between devices  557 us (84%)
  local copies, waits for them, and re-layouts  47 us (7%)
  starting transfers between devices  25.5 us (4%)
  other arithmetic  15.9 us (2%)
  between operations  13.4 us (2%)
    pmin x1, waiting for transfers between devices, local(): nearest = lax.pmin(local_min, 'date')  269 us
    all_gather x1, waiting for transfers between devices, local(): lax.all_gather(latest_model_output, 'date', axis=4, tiled=True)  110 us
    reduce_scatter x1, waiting for transfers between devices, local(): lax.psum_scatter(denom, 'date', scatter_dimension=3, tiled=True)  90.3 us
    reduce_scatter x1, waiting for transfers between devices, local(): lax.psum_scatter(numer, 'date', scatter_dimension=3, tiled=True)  84.8 us
    slice x3, local copies, waits for them, and re-layouts, extended(): last = lax.slice_in_dim(x, length - width, length, axis=dim)  25.4 us
    ppermute x2, starting transfers between devices, extended(): before = lax.ppermute(last, axis, up)  21.3 us
  transfers between devices with their start and end apart: 8, of which 5 were waited for; matrix products, arithmetic and copies ran while one was open for 4% of the time, Pallas kernels for 0%

commit v1 on v0

v1 whole, which is shorter than its diff:
```python
import functools
import math

import jax
import jax.numpy as jnp
from jax import lax
from jax.experimental import pallas as pl
from jax.experimental.pallas import tpu as pltpu
from jax.sharding import PartitionSpec as P

MESH = pl.DeviceIdType.MESH
LEADS = 24
REACH = 3
CHUNKS = ((0, 4), (4, 4), (8, 4), (12, 4), (16, 4), (20, 4))
BLOCK = 8
BLOCKS = LEADS // BLOCK


def remote(src, dst, send, recv, device):
    return pltpu.make_async_remote_copy(
        src_ref=src, dst_ref=dst, send_sem=send, recv_sem=recv, device_id=device, device_id_type=MESH
    )


def kernel(
    cur_hbm, arch_hbm, obs_hbm, w_ref, blur_ref, cal_ref, today_ref,
    out_ref,
    cur_in, arch, obs, stage, landed, gath, curr, dw, edge_lo, edge_hi, halo_up, halo_dn, season, parts, other, pack, packed,
    pieces, ends,
    local_sem, arch_sem, pair_sem, z_send, z_recv, y_send, y_recv, c_send, c_recv, h_send, h_recv, p_send, p_recv,
    r_send, r_recv, e_send, e_recv,
):
    date, tile = lax.axis_index("date"), lax.axis_index("tile")
    row, depth, core = date // 8, (date // 2) % 4, date % 2
    chip = row * 4 + depth
    tiles = 8

    def at(dy, dz):
        return ((((row + dy) % 4) * 4 + (depth + dz) % 4) * 2 + core, tile)

    def chip_at(dy, dz):
        return ((row + dy) % 4) * 4 + (depth + dz) % 4

    partner = (date + 1 - 2 * core, tile)
    others = [(dy, dz) for dy in range(4) for dz in range(4) if (dy, dz) != (0, 0)]

    load_cur = pltpu.make_async_copy(cur_hbm, cur_in, local_sem.at[0])
    load_cur.start()
    barrier = pltpu.get_barrier_semaphore()
    for dy, dz in others:
        pl.semaphore_signal(barrier, inc=1, device_id=at(dy, dz), device_id_type=MESH)
    pl.semaphore_signal(barrier, inc=1, device_id=partner, device_id_type=MESH)

    @pl.when(tile > 0)
    def _():
        pl.semaphore_signal(barrier, inc=1, device_id=(date, tile - 1), device_id_type=MESH)

    @pl.when(tile < tiles - 1)
    def _():
        pl.semaphore_signal(barrier, inc=1, device_id=(date, tile + 1), device_id_type=MESH)

    loads = []
    for j, (t0, n) in enumerate(CHUNKS):
        copy = pltpu.make_async_copy(arch_hbm.at[:, pl.ds(t0, n)], arch.at[:, pl.ds(t0, n)], arch_sem.at[j])
        copy.start()
        loads.append(copy)
    load_obs = pltpu.make_async_copy(obs_hbm, obs, local_sem.at[1])
    load_obs.start()

    load_cur.wait()
    for x in range(4):
        for mine in range(2):
            cycle = core if mine else 1 - core
            values = cur_in[cycle, :, :, x, :].reshape(128, LEADS).T
            if mine:
                gath[:, chip, core * 4 + x, :] = values
            else:
                stage[:, x, :] = values

    pl.semaphore_wait(barrier, 16 + jnp.where(tile > 0, 1, 0) + jnp.where(tile < tiles - 1, 1, 0))

    pair = remote(stage, landed, pair_sem.at[0], pair_sem.at[1], partner)
    pair.start()

    zero = jnp.zeros((8, 128), jnp.float32)
    for k in range(REACH):
        for side in (k, LEADS + REACH + k):
            for i in range(8):
                dw[side, i] = zero
            halo_up[side] = zero
            halo_dn[side] = zero

    @pl.when(tile == 0)
    def _():
        for t in range(LEADS):
            halo_up[REACH + t] = zero

    @pl.when(tile == tiles - 1)
    def _():
        for t in range(LEADS):
            halo_dn[REACH + t] = zero

    sub = lax.broadcasted_iota(jnp.int32, (8, 128), 0)
    lane = lax.broadcasted_iota(jnp.int32, (8, 128), 1)
    days = jnp.zeros((8, 128), jnp.float32)
    for i in range(8):
        gap = (cal_ref[i % 4] - today_ref[i // 4]).astype(jnp.float32)
        days = jnp.where(sub == i, gap, days)
    season[...] = 0.5 * (1.0 - jnp.cos(2.0 * math.pi * days / 365.0))

    pair.wait_recv()
    for x in range(4):
        gath[:, chip, (1 - core) * 4 + x, :] = landed[:, x, :]

    def z_copy(j, dz):
        t0, n = CHUNKS[j]
        return remote(
            gath.at[pl.ds(t0, n), chip], gath.at[pl.ds(t0, n), chip],
            z_send.at[j, dz - 1], z_recv.at[j, dz - 1], at(0, dz),
        )

    def z_wait(j, dz):
        t0, n = CHUNKS[j]
        here = gath.at[pl.ds(t0, n), chip_at(0, 4 - dz)]
        remote(here, here, z_send.at[j, dz - 1], z_recv.at[j, dz - 1], at(0, dz)).wait_recv()

    def y_copy(j, dy):
        t0, n = CHUNKS[j]
        plane = gath.at[pl.ds(t0, n), pl.ds(row * 4, 4)]
        return remote(plane, plane, y_send.at[j, dy - 1], y_recv.at[j, dy - 1], at(dy, 0))

    def y_wait(j, dy):
        t0, n = CHUNKS[j]
        plane = gath.at[pl.ds(t0, n), pl.ds(((row + 4 - dy) % 4) * 4, 4)]
        remote(plane, plane, y_send.at[j, dy - 1], y_recv.at[j, dy - 1], at(dy, 0)).wait_recv()

    def c_copy(j, cycle):
        t0, n = CHUNKS[j]
        block = curr.at[cycle, pl.ds(t0, n)]
        return remote(block, block, c_send.at[j], c_recv.at[j], partner)

    def h_copy(j, up):
        t0, n = CHUNKS[j]
        if up:
            return remote(
                edge_hi.at[pl.ds(t0, n)], halo_up.at[pl.ds(REACH + t0, n)], h_send.at[j, 0], h_recv.at[j, 0], (date, tile + 1)
            )
        return remote(
            edge_lo.at[pl.ds(t0, n)], halo_dn.at[pl.ds(REACH + t0, n)], h_send.at[j, 1], h_recv.at[j, 1], (date, tile - 1)
        )

    def p_copy(b):
        return remote(
            parts.at[1 - core, pl.ds(b * BLOCK, BLOCK)], other.at[pl.ds(b * BLOCK, BLOCK)], p_send.at[b], p_recv.at[b], partner
        )

    def r_copy(b, o):
        dy, dz = others[o]
        return remote(packed.at[b, chip_at(dy, dz)], pieces.at[b, o], r_send.at[b], r_recv.at[b], at(dy, dz))

    for j in range(len(CHUNKS)):
        for dz in (2, 1, 3):
            z_copy(j, dz).start()
    for j in range(len(CHUNKS)):
        for dz in (1, 3, 2):
            z_wait(j, dz)
        for dy in (2, 1, 3):
            y_copy(j, dy).start()

    def transpose(j):
        t0, n = CHUNKS[j]
        for dy in (1, 3, 2):
            y_wait(j, dy)

        def turn(t, carry):
            curr[core, t] = gath[t].reshape(128, 128).T.reshape(16, 8, 128)
            return carry

        lax.fori_loop(t0, t0 + n, turn, 0)
        c_copy(j, core).start()

    def differences(j):
        t0, n = CHUNKS[j]
        loads[j].wait()
        c_copy(j, 1 - core).wait_recv()

        def one(t, carry):
            for d in range(4):
                sums = [None, None]
                for p in range(16):
                    past = arch[d, t, p]
                    for c in range(2):
                        gap = curr[c, t, p] - past
                        term = gap * gap * w_ref[p]
                        sums[c] = term if p == 0 else sums[c] + term
                for c in range(2):
                    v = sums[c]
                    v = (
                        v
                        + jnp.where(lane > 0, pltpu.roll(v, 1, 1), 0.0)
                        + jnp.where(lane < 127, pltpu.roll(v, 127, 1), 0.0)
                    )
                    i = c * 4 + d
                    dw[t + REACH, i] = v
                    edge_lo[t, pl.ds(i, 1)] = v[0:1]
                    edge_hi[t, pl.ds(i, 1)] = v[7:8]
            return carry

        lax.fori_loop(t0, t0 + n, one, 0)

        @pl.when(tile < tiles - 1)
        def _():
            h_copy(j, True).start()

        @pl.when(tile > 0)
        def _():
            h_copy(j, False).start()

    done = [0]
    sent = [0]

    def scores(j):
        t0, n = CHUNKS[j]
        last = j == len(CHUNKS) - 1
        stop = LEADS if last else t0 + n - REACH
        if j == 0:
            load_obs.wait()

        @pl.when(tile > 0)
        def _():
            h_copy(j, True).wait_recv()

        @pl.when(tile < tiles - 1)
        def _():
            h_copy(j, False).wait_recv()

        def one(t, carry):
            above, below = halo_up[t], halo_dn[t]
            for k in range(1, 2 * REACH + 1):
                above = above + halo_up[t + k]
                below = below + halo_dn[t + k]
            spread = blur_ref[t]
            for c in range(2):
                dist = []
                for d in range(4):
                    i = c * 4 + d
                    v = dw[t, i]
                    for k in range(1, 2 * REACH + 1):
                        v = v + dw[t + k, i]
                    up = jnp.where(sub == 0, jnp.broadcast_to(above[i : i + 1], (8, 128)), pltpu.roll(v, 1, 0))
                    down = jnp.where(sub == 7, jnp.broadcast_to(below[i : i + 1], (8, 128)), pltpu.roll(v, 7, 0))
                    v = (v + up + down) * (1.0 / (16.0 * 9.0 * (2 * REACH + 1)))
                    dist.append(v + jnp.broadcast_to(season[pl.ds(i, 1)], (8, 128)))
                low = jnp.minimum(jnp.minimum(dist[0], dist[1]), jnp.minimum(dist[2], dist[3]))
                den = num = None
                for d in range(4):
                    e = jnp.exp((low - dist[d]) / spread)
                    f = e * obs[d, t]
                    den = e if d == 0 else den + e
                    num = f if d == 0 else num + f
                parts[c, t, 0] = low - spread * jnp.log(den)
                parts[c, t, 1] = num / den
            return carry

        lax.fori_loop(done[0], stop, one, 0)
        done[0] = stop
        while sent[0] < BLOCKS and done[0] >= (sent[0] + 1) * BLOCK:
            p_copy(sent[0]).start()
            sent[0] += 1

    def combine(b):
        p_copy(b).wait_recv()

        def one(s, carry):
            t = b * BLOCK + s
            spread = blur_ref[t]
            a0, r0 = parts[core, t, 0], parts[core, t, 1]
            a1, r1 = other[t, 0], other[t, 1]
            low = jnp.minimum(a0, a1)
            e0, e1 = jnp.exp((low - a0) / spread), jnp.exp((low - a1) / spread)
            den = e0 + e1
            pack[0, :, s, :] = low - spread * jnp.log(den)
            pack[1, :, s, :] = (e0 * r0 + e1 * r1) / den
            return carry

        lax.fori_loop(0, BLOCK, one, 0)
        packed[b] = pack[...].reshape(128, 128).T.reshape(16, 8, 128)
        for o in range(15):
            r_copy(b, o).start()

    combined = 0
    for j in range(len(CHUNKS)):
        transpose(j)
        if j > 0:
            before = sent[0]
            while combined < before:
                combine(combined)
                combined += 1
            scores(j - 1)
        differences(j)
    scores(len(CHUNKS) - 1)
    while combined < BLOCKS:
        combine(combined)
        combined += 1

    for b in range(BLOCKS):
        here = pieces.at[b]
        remote(here, here, r_send.at[b], r_recv.at[b], partner).wait_recv()
        spread = jnp.zeros((8, 128), jnp.float32)
        for s in range(BLOCK):
            spread = jnp.where(lane % BLOCK == s, blur_ref[b * BLOCK + s], spread)
        terms = [packed[b, chip]] + [pieces[b, o] for o in range(15)]
        low = functools.reduce(jnp.minimum, terms)
        den = num = None
        for i, v in enumerate(terms):
            e = jnp.exp((low - v) / spread)
            f = pltpu.roll(e, 64, 1) * v
            den = e if i == 0 else den + e
            num = f if i == 0 else num + f
        ends[core, b] = num / pltpu.roll(den, 64, 1)

    swap = remote(ends.at[core], ends.at[core], e_send, e_recv, partner)
    swap.start()
    other_ends = remote(ends.at[1 - core], ends.at[1 - core], e_send, e_recv, partner)
    other_ends.wait_recv()
    for c in range(2):
        blocks = []
        for b in range(BLOCKS):
            v = ends[c, b]
            blocks.append(jnp.where(core == 0, v, pltpu.roll(v, 4, 0)))
        for y in range(8):
            v = jnp.zeros((8, 128), jnp.float32)
            for b in range(BLOCKS):
                shift = (b * BLOCK - 64 - y * BLOCK) % 128
                moved = blocks[b] if shift == 0 else pltpu.roll(blocks[b], shift, 1)
                v = jnp.where(lane // BLOCK == b, moved, v)
            out_ref[c, y] = v[0:4, 0:LEADS]

    pair.wait_send()
    swap.wait_send()
    for j in range(len(CHUNKS)):
        for d in (1, 2, 3):
            z_copy(j, d).wait_send()
            y_copy(j, d).wait_send()
        c_copy(j, core).wait_send()

    @pl.when(tile < tiles - 1)
    def _():
        for j in range(len(CHUNKS)):
            h_copy(j, True).wait_send()

    @pl.when(tile > 0)
    def _():
        for j in range(len(CHUNKS)):
            h_copy(j, False).wait_send()

    for b in range(BLOCKS):
        p_copy(b).wait_send()
        here = pieces.at[b]
        remote(here, here, r_send.at[b], r_recv.at[b], partner).wait_send()


def local(current, archive, reports, weights, blur, calendar, today):
    count = len(CHUNKS)
    f32 = jnp.float32
    dma = pltpu.SemaphoreType.DMA
    leads = LEADS + 2 * REACH
    out = pl.pallas_call(
        kernel,
        out_shape=jax.ShapeDtypeStruct((2, 8, 4, LEADS), f32),
        in_specs=[pl.BlockSpec(memory_space=pl.ANY)] * 3 + [pl.BlockSpec(memory_space=pltpu.SMEM)] * 4,
        out_specs=pl.BlockSpec(memory_space=pltpu.VMEM),
        scratch_shapes=[
            pltpu.VMEM((2, 16, 8, 4, LEADS), f32),
            pltpu.VMEM((4, LEADS, 16, 8, 128), f32),
            pltpu.VMEM((4, LEADS, 8, 128), f32),
            pltpu.VMEM((LEADS, 4, 128), f32),
            pltpu.VMEM((LEADS, 4, 128), f32),
            pltpu.VMEM((LEADS, 16, 8, 128), f32),
            pltpu.VMEM((2, LEADS, 16, 8, 128), f32),
            pltpu.VMEM((leads, 8, 8, 128), f32),
            pltpu.VMEM((LEADS, 8, 128), f32),
            pltpu.VMEM((LEADS, 8, 128), f32),
            pltpu.VMEM((leads, 8, 128), f32),
            pltpu.VMEM((leads, 8, 128), f32),
            pltpu.VMEM((8, 128), f32),
            pltpu.VMEM((2, LEADS, 2, 8, 128), f32),
            pltpu.VMEM((LEADS, 2, 8, 128), f32),
            pltpu.VMEM((2, 8, BLOCK, 128), f32),
            pltpu.VMEM((BLOCKS, 16, 8, 128), f32),
            pltpu.VMEM((BLOCKS, 15, 8, 128), f32),
            pltpu.VMEM((2, BLOCKS, 8, 128), f32),
            dma((2,)),
            dma((count,)),
            dma((2,)),
            dma((count, 3)), dma((count, 3)),
            dma((count, 3)), dma((count, 3)),
            dma((count,)), dma((count,)),
            dma((count, 2)), dma((count, 2)),
            dma((BLOCKS,)), dma((BLOCKS,)),
            dma((BLOCKS,)), dma((BLOCKS,)),
            dma, dma,
        ],
        compiler_params=pltpu.CompilerParams(
            collective_id=0, has_side_effects=True, vmem_limit_bytes=40 * 2**20
        ),
    )(jnp.transpose(current, (0, 2, 3, 4, 1)), archive, reports, weights, blur, calendar, today)
    return jnp.transpose(out, (0, 3, 1, 2))


def solution(mesh):
    placed = (
        P(None, None, None, "tile", "date"),
        P("date", None, None, "tile", None),
        P("date", None, "tile", None),
        P(),
        P(),
        P("date"),
        P(),
    )
    return jax.shard_map(
        local, mesh=mesh, in_specs=placed, out_specs=P(None, None, "tile", "date"), check_vma=False
    )
```

time: 661 us -> 70.2 us (0.11)
  waiting for transfers between devices: 557 us -> 0 us
  Pallas kernels: 0 us -> 61.9 us
  local copies, waits for them, and re-layouts: 47 us -> 8.06 us
  starting transfers between devices: 25.5 us -> 0 us
  other arithmetic: 15.9 us -> 0 us
  between operations: 13.4 us -> 0.02 us
    pmin x1 -> x0, waiting for transfers between devices: 269 us -> none  [local(): nearest = lax.pmin(local_min, 'date')]
    reduce_scatter x2 -> x0, waiting for transfers between devices: 175 us -> none  [the longest x1 90.3 us: local(): lax.psum_scatter(denom, 'date', scatter_dimension=3, tiled=True)]
    all_gather x1 -> x0, waiting for transfers between devices: 110 us -> none  [local(): lax.all_gather(latest_model_output, 'date', axis=4, tiled=True)]
    pallas_call x0 -> x1, Pallas kernels: none -> 61.9 us  [local(): pl.pallas_call(kernel, out_shape=jax.ShapeDtypeStruct((2, 8, 4, LEADS), f...]
    slice x5 -> x0, local copies, waits for them, and re-layouts: 28.1 us -> none  [the longest x3 25.4 us: extended(): last = lax.slice_in_dim(x, length - width, length, axis=dim)]
    ppermute x4 -> x0, starting transfers between devices: 25.3 us -> none  [the longest x2 21.3 us: extended(): before = lax.ppermute(last, axis, up)]
    all_gather x1 -> x0, local copies, waits for them, and re-layouts: 11.7 us -> none  [local(): lax.all_gather(latest_model_output, 'date', axis=4, tiled=True)]
    reduce_sum x2 -> x0, other arithmetic: 9.23 us -> none  [the longest x1 8 us: cycle_distance(): jnp.sum(feature_discrepancy * feature_discrepancy * input_variable_scalin...]
  transfers between devices with their start and end apart: 8 -> 0, of which waited for: 5 -> 0; matrix products, arithmetic and copies ran while one was open for 4% -> 0% of each run, Pallas kernels for 0% -> 0%
where the time goes in v1:
time: 70.2 us; the launch traced here: 70 us
  Pallas kernels  61.9 us (88%)
  local copies, waits for them, and re-layouts  8.06 us (11%)
    pallas_call x1, Pallas kernels, local(): pl.pallas_call(kernel, out_shape=jax.ShapeDtypeStruct((2, 8, 4, LEADS), f...  61.9 us
    unnamed x15, local copies, waits for them, and re-layouts  8.06 us

profile of v1, /device:TPU:7, one launch (start us, length us, event | category | flops | bytes accessed | tf_op | source)
XLA Modules:
  0.0 70.0 jit_solution(6729807088847093483)
XLA Ops:
  0.0 0.0 copy-start
  0.0 2.8 %copy-done = f32[4,24,16,8,128]{4,3,2,1,0:T(8,128)S(1)} copy-done((f32[4,24,16,8,128]{4,3,2,1,0:T(8,128)S(1)}, f32[4,24,16,8,128]{4,3,2,1,0:T(8,128)}, u32[]{:S(2)}) %copy-start) | copy-done | bytes 6291480
  2.8 0.0 copy-start.1
  2.8 1.0 %copy-done.1 = f32[2,24,16,8,4]{1,4,3,2,0:T(4,128)S(1)} copy-done((f32[2,24,16,8,4]{1,4,3,2,0:T(4,128)S(1)}, f32[2,24,16,8,4]{1,4,3,2,0:T(4,128)}, u32[]{:S(2)}) %copy-start.1) | copy-done | bytes 98328
  3.8 0.0 copy-start.2
  3.8 1.0 %copy-done.2 = f32[4,24,8,128]{3,2,1,0:T(8,128)S(1)} copy-done((f32[4,24,8,128]{3,2,1,0:T(8,128)S(1)}, f32[4,24,8,128]{3,2,1,0:T(8,128)}, u32[]{:S(2)}) %copy-start.2) | copy-done | bytes 393240
  4.8 0.0 copy-start.3
  4.8 0.7 copy-done.3
  5.5 0.0 copy-start.4
  5.5 0.7 copy-done.4
  6.1 0.0 copy-start.5
  6.1 0.7 copy-done.5
  6.8 0.0 copy-start.6
  6.8 0.7 copy-done.6
  7.4 61.9 %shard_map.73 = f32[2,8,4,24]{3,2,1,0:T(4,128)S(1)} custom-call(f32[2,16,8,4,24]{4,3,2,1,0:T(4,128)S(1)} %bitcast.2, f32[4,24,16,8,128]{4,3,2,1,0:T(8,128)S(1)} %copy-done, f32[4,24,8,128]{3,2,1,0:T(8,128)S(1)} %copy-done.2, f32[16]{0:T(128)S(1)} %copy-done.3, f32[24]{0:T(128)S(1)} %copy-done.4, s32[4]{0:T(128)S(1)} %copy-done.5, s32[2]{0:T(128)S(1)} %copy-done.6), custom_call_target="tpu_custom_call" | custom-call | tf_op jit(solution)/shard_map/pallas_call | solution.py:368
  69.4 0.6 copy.9
Async XLA Ops:
  0.0 2.8 %copy-start = (f32[4,24,16,8,128]{4,3,2,1,0:T(8,128)S(1)}, f32[4,24,16,8,128]{4,3,2,1,0:T(8,128)}, u32[]{:S(2)}) copy-start(f32[4,24,16,8,128]{4,3,2,1,0:T(8,128)} %arch_hbm.1) | copy-start | bytes 18874372
  2.8 1.0 %copy-start.1 = (f32[2,24,16,8,4]{1,4,3,2,0:T(4,128)S(1)}, f32[2,24,16,8,4]{1,4,3,2,0:T(4,128)}, u32[]{:S(2)}) copy-start(f32[2,24,16,8,4]{1,4,3,2,0:T(4,128)} %param.7) | copy-start | bytes 294916
  3.8 1.0 %copy-start.2 = (f32[4,24,8,128]{3,2,1,0:T(8,128)S(1)}, f32[4,24,8,128]{3,2,1,0:T(8,128)}, u32[]{:S(2)}) copy-start(f32[4,24,8,128]{3,2,1,0:T(8,128)} %obs_hbm.1) | copy-start | bytes 1179652
  4.8 0.7 copy-start.3
  5.5 0.7 copy-start.4
  6.1 0.7 copy-start.5
  6.8 0.7 copy-start.6

commit v2 on v1

--- a/solution.py
+++ b/solution.py
@@ -11,7 +11,10 @@
 MESH = pl.DeviceIdType.MESH
 LEADS = 24
 REACH = 3
-CHUNKS = ((0, 4), (4, 4), (8, 4), (12, 4), (16, 4), (20, 4))
+CHUNKS = ((6, 6, False), (12, 6, False), (18, 6, False), (0, 6, True))
+STEPS = (
+    ("F", 3), ("F", 0), ("F", 1), ("R", 0), ("F", 2), ("R", 1), ("T", 0), ("R", 2), ("T", 1), ("D", 0), ("T", 3), ("D", 1), ("S", 0), ("T", 2), ("D", 3), ("S", 1), ("D", 2), ("S", 3), ("S", 2),
+)
 BLOCK = 8
 BLOCKS = LEADS // BLOCK
 
@@ -23,8 +26,9 @@
 
 
 def kernel(
-    cur_hbm, arch_hbm, obs_hbm, w_ref, blur_ref, cal_ref, today_ref,
+    cur_hbm, arch_hbm, obs_hbm, w_hbm, blur_hbm, cal_hbm, today_hbm,
     out_ref,
+    w_ref, blur_ref, cal_ref, today_ref,
     cur_in, arch, obs, stage, landed, gath, curr, dw, edge_lo, edge_hi, halo_up, halo_dn, season, parts, other, pack, packed,
     pieces, ends,
     local_sem, arch_sem, pair_sem, z_send, z_recv, y_send, y_recv, c_send, c_recv, h_send, h_recv, p_send, p_recv,
@@ -46,9 +50,15 @@
 
     load_cur = pltpu.make_async_copy(cur_hbm, cur_in, local_sem.at[0])
     load_cur.start()
+    small = []
+    for i, (src, dst) in enumerate(((w_hbm, w_ref), (blur_hbm, blur_ref), (cal_hbm, cal_ref), (today_hbm, today_ref))):
+        copy = pltpu.make_async_copy(src, dst, local_sem.at[2 + i])
+        copy.start()
+        small.append(copy)
     barrier = pltpu.get_barrier_semaphore()
-    for dy, dz in others:
-        pl.semaphore_signal(barrier, inc=1, device_id=at(dy, dz), device_id_type=MESH)
+    for step in (1, 3, 2):
+        pl.semaphore_signal(barrier, inc=1, device_id=at(0, step), device_id_type=MESH)
+        pl.semaphore_signal(barrier, inc=1, device_id=at(step, 0), device_id_type=MESH)
     pl.semaphore_signal(barrier, inc=1, device_id=partner, device_id_type=MESH)
 
     @pl.when(tile > 0)
@@ -60,7 +70,7 @@
         pl.semaphore_signal(barrier, inc=1, device_id=(date, tile + 1), device_id_type=MESH)
 
     loads = []
-    for j, (t0, n) in enumerate(CHUNKS):
+    for j, (t0, n, _) in enumerate(CHUNKS):
         copy = pltpu.make_async_copy(arch_hbm.at[:, pl.ds(t0, n)], arch.at[:, pl.ds(t0, n)], arch_sem.at[j])
         copy.start()
         loads.append(copy)
@@ -73,11 +83,11 @@
             cycle = core if mine else 1 - core
             values = cur_in[cycle, :, :, x, :].reshape(128, LEADS).T
             if mine:
-                gath[:, chip, core * 4 + x, :] = values
+                gath[:, row, depth, core * 4 + x, :] = values
             else:
                 stage[:, x, :] = values
 
-    pl.semaphore_wait(barrier, 16 + jnp.where(tile > 0, 1, 0) + jnp.where(tile < tiles - 1, 1, 0))
+    pl.semaphore_wait(barrier, 7 + jnp.where(tile > 0, 1, 0) + jnp.where(tile < tiles - 1, 1, 0))
 
     pair = remote(stage, landed, pair_sem.at[0], pair_sem.at[1], partner)
     pair.start()
@@ -100,6 +110,8 @@
         for t in range(LEADS):
             halo_dn[REACH + t] = zero
 
+    for copy in small:
+        copy.wait()
     sub = lax.broadcasted_iota(jnp.int32, (8, 128), 0)
     lane = lax.broadcasted_iota(jnp.int32, (8, 128), 1)
     days = jnp.zeros((8, 128), jnp.float32)
@@ -110,37 +122,61 @@
 
     pair.wait_recv()
     for x in range(4):
-        gath[:, chip, (1 - core) * 4 + x, :] = landed[:, x, :]
-
-    def z_copy(j, dz):
-        t0, n = CHUNKS[j]
-        return remote(
-            gath.at[pl.ds(t0, n), chip], gath.at[pl.ds(t0, n), chip],
-            z_send.at[j, dz - 1], z_recv.at[j, dz - 1], at(0, dz),
-        )
-
-    def z_wait(j, dz):
-        t0, n = CHUNKS[j]
-        here = gath.at[pl.ds(t0, n), chip_at(0, 4 - dz)]
-        remote(here, here, z_send.at[j, dz - 1], z_recv.at[j, dz - 1], at(0, dz)).wait_recv()
-
-    def y_copy(j, dy):
-        t0, n = CHUNKS[j]
-        plane = gath.at[pl.ds(t0, n), pl.ds(row * 4, 4)]
-        return remote(plane, plane, y_send.at[j, dy - 1], y_recv.at[j, dy - 1], at(dy, 0))
-
-    def y_wait(j, dy):
-        t0, n = CHUNKS[j]
-        plane = gath.at[pl.ds(t0, n), pl.ds(((row + 4 - dy) % 4) * 4, 4)]
-        remote(plane, plane, y_send.at[j, dy - 1], y_recv.at[j, dy - 1], at(dy, 0)).wait_recv()
+        gath[:, row, depth, (1 - core) * 4 + x, :] = landed[:, x, :]
+
+    def part(j, y, z):
+        t0, n, _ = CHUNKS[j]
+        return gath.at[pl.ds(t0, n), y, z]
+
+    def first(j, d):
+        mine = part(j, row, depth)
+        to = at(d, 0) if CHUNKS[j][2] else at(0, d)
+        return remote(mine, mine, z_send.at[j, d - 1], z_recv.at[j, d - 1], to)
+
+    def first_wait(j, d):
+        here = part(j, (row + 4 - d) % 4, depth) if CHUNKS[j][2] else part(j, row, (depth + 4 - d) % 4)
+        remote(here, here, z_send.at[j, d - 1], z_recv.at[j, d - 1], partner).wait_recv()
+
+    every = slice(None)
+    halves = (pl.ds(0, 2), pl.ds(2, 2))
+
+    def second(j, d):
+        if CHUNKS[j][2]:
+            t0, n, _ = CHUNKS[j]
+            line = gath.at[pl.ds(t0, n), every, depth]
+            return remote(line, line, y_send.at[j, d - 1], y_recv.at[j, d - 1], at(0, d))
+        if d == 1 or d == 3:
+            plane = part(j, row, every)
+            return remote(plane, plane, y_send.at[j, d - 1], y_recv.at[j, d - 1], at(d, 0))
+        raise ValueError(d)
+
+    def second_wait(j, d):
+        if CHUNKS[j][2]:
+            t0, n, _ = CHUNKS[j]
+            here = gath.at[pl.ds(t0, n), every, (depth + 4 - d) % 4]
+        else:
+            here = part(j, (row + 4 - d) % 4, every)
+        remote(here, here, y_send.at[j, d - 1], y_recv.at[j, d - 1], partner).wait_recv()
+
+    def forward(j, up):
+        if up:
+            half = part(j, (row + 3) % 4, halves[0])
+            return remote(half, half, y_send.at[j, 1], y_recv.at[j, 1], at(1, 0))
+        half = part(j, (row + 1) % 4, halves[1])
+        return remote(half, half, y_send.at[j, 3], y_recv.at[j, 3], at(3, 0))
+
+    def forward_wait(j, up):
+        half = part(j, (row + 2) % 4, halves[0 if up else 1])
+        sem = 1 if up else 3
+        remote(half, half, y_send.at[j, sem], y_recv.at[j, sem], partner).wait_recv()
 
     def c_copy(j, cycle):
-        t0, n = CHUNKS[j]
+        t0, n, _ = CHUNKS[j]
         block = curr.at[cycle, pl.ds(t0, n)]
         return remote(block, block, c_send.at[j], c_recv.at[j], partner)
 
     def h_copy(j, up):
-        t0, n = CHUNKS[j]
+        t0, n, _ = CHUNKS[j]
         if up:
             return remote(
                 edge_hi.at[pl.ds(t0, n)], halo_up.at[pl.ds(REACH + t0, n)], h_send.at[j, 0], h_recv.at[j, 0], (date, tile + 1)
@@ -158,19 +194,31 @@
         dy, dz = others[o]
         return remote(packed.at[b, chip_at(dy, dz)], pieces.at[b, o], r_send.at[b], r_recv.at[b], at(dy, dz))
 
-    for j in range(len(CHUNKS)):
-        for dz in (2, 1, 3):
-            z_copy(j, dz).start()
-    for j in range(len(CHUNKS)):
-        for dz in (1, 3, 2):
-            z_wait(j, dz)
-        for dy in (2, 1, 3):
-            y_copy(j, dy).start()
+    plain = [j for j in range(len(CHUNKS)) if not CHUNKS[j][2]]
+    turned = [j for j in range(len(CHUNKS)) if CHUNKS[j][2]]
+    for j in turned + plain:
+        for d in (2, 1, 3):
+            first(j, d).start()
+    def relay(j):
+        second_wait(j, 1)
+        forward(j, True).start()
+        second_wait(j, 3)
+        forward(j, False).start()
+
+    def onward(j):
+        for d in (1, 3, 2):
+            first_wait(j, d)
+        for d in (2, 1, 3) if CHUNKS[j][2] else (1, 3):
+            second(j, d).start()
 
     def transpose(j):
-        t0, n = CHUNKS[j]
-        for dy in (1, 3, 2):
-            y_wait(j, dy)
+        t0, n, _ = CHUNKS[j]
+        if CHUNKS[j][2]:
+            for d in (1, 3, 2):
+                second_wait(j, d)
+        else:
+            forward_wait(j, True)
+            forward_wait(j, False)
 
         def turn(t, carry):
             curr[core, t] = gath[t].reshape(128, 128).T.reshape(16, 8, 128)
@@ -180,7 +228,7 @@
         c_copy(j, core).start()
 
     def differences(j):
-        t0, n = CHUNKS[j]
+        t0, n, _ = CHUNKS[j]
         loads[j].wait()
         c_copy(j, 1 - core).wait_recv()
 
@@ -216,14 +264,11 @@
         def _():
             h_copy(j, False).start()
 
-    done = [0]
-    sent = [0]
+    scored, sent, seen = set(), [0], set()
 
     def scores(j):
-        t0, n = CHUNKS[j]
-        last = j == len(CHUNKS) - 1
-        stop = LEADS if last else t0 + n - REACH
-        if j == 0:
+        t0, n, _ = CHUNKS[j]
+        if not seen:
             load_obs.wait()
 
         @pl.when(tile > 0)
@@ -240,6 +285,7 @@
                 above = above + halo_up[t + k]
                 below = below + halo_dn[t + k]
             spread = blur_ref[t]
+            inverse = 1.0 / jnp.full((8, 128), spread, jnp.float32)
             for c in range(2):
                 dist = []
                 for d in range(4):
@@ -254,7 +300,7 @@
                 low = jnp.minimum(jnp.minimum(dist[0], dist[1]), jnp.minimum(dist[2], dist[3]))
                 den = num = None
                 for d in range(4):
-                    e = jnp.exp((low - dist[d]) / spread)
+                    e = jnp.exp((low - dist[d]) * inverse)
                     f = e * obs[d, t]
                     den = e if d == 0 else den + e
                     num = f if d == 0 else num + f
@@ -262,9 +308,19 @@
                 parts[c, t, 1] = num / den
             return carry
 
-        lax.fori_loop(done[0], stop, one, 0)
-        done[0] = stop
-        while sent[0] < BLOCKS and done[0] >= (sent[0] + 1) * BLOCK:
+        seen.update(range(t0, t0 + n))
+        ready = [
+            t for t in range(LEADS)
+            if t not in scored and all(u in seen for u in range(max(t - REACH, 0), min(t + REACH + 1, LEADS)))
+        ]
+        while ready:
+            stop = ready[0] + 1
+            while stop in ready:
+                stop += 1
+            lax.fori_loop(ready[0], stop, one, 0)
+            scored.update(range(ready[0], stop))
+            ready = [t for t in ready if t >= stop]
+        while sent[0] < BLOCKS and all(t in scored for t in range(sent[0] * BLOCK, (sent[0] + 1) * BLOCK)):
             p_copy(sent[0]).start()
             sent[0] += 1
 
@@ -288,20 +344,21 @@
         for o in range(15):
             r_copy(b, o).start()
 
+    acts = {"F": onward, "R": relay, "T": transpose, "D": differences, "S": scores}
     combined = 0
-    for j in range(len(CHUNKS)):
-        transpose(j)
-        if j > 0:
-            before = sent[0]
-            while combined < before:
+    for kind, j in STEPS:
+        due = sent[0]
+        acts[kind](j)
+        if kind != "R":
+            while combined < due:
                 combine(combined)
                 combined += 1
-            scores(j - 1)
-        differences(j)
-    scores(len(CHUNKS) - 1)
     while combined < BLOCKS:
         combine(combined)
         combined += 1
+
+    def e_copy(b, cycle):
+        return remote(ends.at[cycle, b], ends.at[cycle, b], e_send.at[b], e_recv.at[b], partner)
 
     for b in range(BLOCKS):
         here = pieces.at[b]
@@ -318,11 +375,10 @@
             den = e if i == 0 else den + e
             num = f if i == 0 else num + f
         ends[core, b] = num / pltpu.roll(den, 64, 1)
-
-    swap = remote(ends.at[core], ends.at[core], e_send, e_recv, partner)
-    swap.start()
-    other_ends = remote(ends.at[1 - core], ends.at[1 - core], e_send, e_recv, partner)
-    other_ends.wait_recv()
+        e_copy(b, core).start()
+
+    for b in range(BLOCKS):
+        e_copy(b, 1 - core).wait_recv()
     for c in range(2):
         blocks = []
         for b in range(BLOCKS):
@@ -337,11 +393,14 @@
             out_ref[c, y] = v[0:4, 0:LEADS]
 
     pair.wait_send()
-    swap.wait_send()
     for j in range(len(CHUNKS)):
         for d in (1, 2, 3):
-            z_copy(j, d).wait_send()
-            y_copy(j, d).wait_send()
+            first(j, d).wait_send()
+            if CHUNKS[j][2] or d != 2:
+                second(j, d).wait_send()
+        if not CHUNKS[j][2]:
+            forward(j, True).wait_send()
+            forward(j, False).wait_send()
         c_copy(j, core).wait_send()
 
     @pl.when(tile < tiles - 1)
@@ -356,6 +415,7 @@
 
     for b in range(BLOCKS):
         p_copy(b).wait_send()
+        e_copy(b, core).wait_send()
         here = pieces.at[b]
         remote(here, here, r_send.at[b], r_recv.at[b], partner).wait_send()
 
@@ -368,15 +428,16 @@
     out = pl.pallas_call(
         kernel,
         out_shape=jax.ShapeDtypeStruct((2, 8, 4, LEADS), f32),
-        in_specs=[pl.BlockSpec(memory_space=pl.ANY)] * 3 + [pl.BlockSpec(memory_space=pltpu.SMEM)] * 4,
+        in_specs=[pl.BlockSpec(memory_space=pl.ANY)] * 7,
         out_specs=pl.BlockSpec(memory_space=pltpu.VMEM),
         scratch_shapes=[
+            pltpu.SMEM((16,), f32), pltpu.SMEM((LEADS,), f32), pltpu.SMEM((4,), jnp.int32), pltpu.SMEM((2,), jnp.int32),
             pltpu.VMEM((2, 16, 8, 4, LEADS), f32),
             pltpu.VMEM((4, LEADS, 16, 8, 128), f32),
             pltpu.VMEM((4, LEADS, 8, 128), f32),
             pltpu.VMEM((LEADS, 4, 128), f32),
             pltpu.VMEM((LEADS, 4, 128), f32),
-            pltpu.VMEM((LEADS, 16, 8, 128), f32),
+            pltpu.VMEM((LEADS, 4, 4, 8, 128), f32),
             pltpu.VMEM((2, LEADS, 16, 8, 128), f32),
             pltpu.VMEM((leads, 8, 8, 128), f32),
             pltpu.VMEM((LEADS, 8, 128), f32),
@@ -390,19 +451,19 @@
             pltpu.VMEM((BLOCKS, 16, 8, 128), f32),
             pltpu.VMEM((BLOCKS, 15, 8, 128), f32),
             pltpu.VMEM((2, BLOCKS, 8, 128), f32),
-            dma((2,)),
+            dma((6,)),
             dma((count,)),
             dma((2,)),
             dma((count, 3)), dma((count, 3)),
-            dma((count, 3)), dma((count, 3)),
+            dma((count, 4)), dma((count, 4)),
             dma((count,)), dma((count,)),
             dma((count, 2)), dma((count, 2)),
             dma((BLOCKS,)), dma((BLOCKS,)),
             dma((BLOCKS,)), dma((BLOCKS,)),
-            dma, dma,
+            dma((BLOCKS,)), dma((BLOCKS,)),
         ],
         compiler_params=pltpu.CompilerParams(
-            collective_id=0, has_side_effects=True, vmem_limit_bytes=40 * 2**20
+            collective_id=0, has_side_effects=True, vmem_limit_bytes=60 * 2**20
         ),
     )(jnp.transpose(current, (0, 2, 3, 4, 1)), archive, reports, weights, blur, calendar, today)
     return jnp.transpose(out, (0, 3, 1, 2))

time: 70.2 us -> 52.5 us (0.75)
  Pallas kernels: 61.9 us -> 51 us
  local copies, waits for them, and re-layouts: 8.06 us -> 1.38 us
    pallas_call x1, Pallas kernels: 61.9 us -> 51 us  [local(): pl.pallas_call(kernel, out_shape=jax.ShapeDtypeStruct((2, 8, 4, LEADS), f...]
    unnamed x15 -> x1, local copies, waits for them, and re-layouts: 8.06 us -> 1.38 us
where the time goes in v2:
time: 52.5 us; the launch traced here: 52.4 us
  Pallas kernels  51 us (97%)
  local copies, waits for them, and re-layouts  1.38 us (3%)
    pallas_call x1, Pallas kernels, local(): pl.pallas_call(kernel, out_shape=jax.ShapeDtypeStruct((2, 8, 4, LEADS), f...  51 us
    unnamed x1, local copies, waits for them, and re-layouts  1.38 us

profile of v2, /device:TPU:7, one launch (start us, length us, event | category | flops | bytes accessed | tf_op | source)
XLA Modules:
  0.0 52.4 jit_solution(8085496301514725968)
XLA Ops:
  0.0 51.0 %shard_map.73 = f32[2,8,4,24]{3,2,1,0:T(4,128)} custom-call(f32[2,16,8,4,24]{4,3,2,1,0:T(4,128)} %bitcast.2, f32[4,24,16,8,128]{4,3,2,1,0:T(8,128)} %arch_hbm.1, f32[4,24,8,128]{3,2,1,0:T(8,128)} %obs_hbm.1, f32[16]{0:T(128)} %w_hbm.1, f32[24]{0:T(128)} %blur_hbm.1, s32[4]{0:T(128)} %cal_hbm.1, s32[2]{0:T(128)} %today_hbm.1), custom_call_target="tpu_custom_call" | custom-call | tf_op jit(solution)/shard_map/pallas_call | solution.py:428
  51.0 1.4 %copy.9 = f32[2,24,8,4]{1,3,2,0:T(4,128)} copy(f32[2,24,8,4]{1,3,2,0:T(4,128)} %bitcast.3) | data formatting | bytes 12288

commit v3 on v2

--- a/solution.py
+++ b/solution.py
@@ -11,9 +11,9 @@
 MESH = pl.DeviceIdType.MESH
 LEADS = 24
 REACH = 3
-CHUNKS = ((6, 6, False), (12, 6, False), (18, 6, False), (0, 6, True))
+CHUNKS = ((6, 6, False, True), (12, 6, False, True), (18, 6, False, True), (0, 6, True, False))
 STEPS = (
-    ("F", 3), ("F", 0), ("F", 1), ("R", 0), ("F", 2), ("R", 1), ("T", 0), ("R", 2), ("T", 1), ("D", 0), ("T", 3), ("D", 1), ("S", 0), ("T", 2), ("D", 3), ("S", 1), ("D", 2), ("S", 3), ("S", 2),
+    ("F", 3), ("F", 0), ("F", 1), ("R", 0), ("F", 2), ("R", 1), ("T", 0), ("R", 2), ("T", 1), ("D", 0), ("T", 3), ("D", 1), ("T", 2), ("D", 3), ("S", 0), ("D", 2), ("S", 1), ("S", 3), ("S", 2),
 )
 BLOCK = 8
 BLOCKS = LEADS // BLOCK
@@ -70,7 +70,7 @@
         pl.semaphore_signal(barrier, inc=1, device_id=(date, tile + 1), device_id_type=MESH)
 
     loads = []
-    for j, (t0, n, _) in enumerate(CHUNKS):
+    for j, (t0, n, _, _) in enumerate(CHUNKS):
         copy = pltpu.make_async_copy(arch_hbm.at[:, pl.ds(t0, n)], arch.at[:, pl.ds(t0, n)], arch_sem.at[j])
         copy.start()
         loads.append(copy)
@@ -125,7 +125,7 @@
         gath[:, row, depth, (1 - core) * 4 + x, :] = landed[:, x, :]
 
     def part(j, y, z):
-        t0, n, _ = CHUNKS[j]
+        t0, n = CHUNKS[j][:2]
         return gath.at[pl.ds(t0, n), y, z]
 
     def first(j, d):
@@ -140,43 +140,37 @@
     every = slice(None)
     halves = (pl.ds(0, 2), pl.ds(2, 2))
 
+    def line(j, d, which):
+        if CHUNKS[j][2]:
+            return part(j, which, (depth + 4 - d) % 4)
+        return part(j, (row + 4 - d) % 4, which)
+
+    def ahead(j, d):
+        return at(0, d) if CHUNKS[j][2] else at(d, 0)
+
     def second(j, d):
-        if CHUNKS[j][2]:
-            t0, n, _ = CHUNKS[j]
-            line = gath.at[pl.ds(t0, n), every, depth]
-            return remote(line, line, y_send.at[j, d - 1], y_recv.at[j, d - 1], at(0, d))
-        if d == 1 or d == 3:
-            plane = part(j, row, every)
-            return remote(plane, plane, y_send.at[j, d - 1], y_recv.at[j, d - 1], at(d, 0))
-        raise ValueError(d)
+        mine = line(j, 0, every)
+        return remote(mine, mine, y_send.at[j, d - 1], y_recv.at[j, d - 1], ahead(j, d))
 
     def second_wait(j, d):
-        if CHUNKS[j][2]:
-            t0, n, _ = CHUNKS[j]
-            here = gath.at[pl.ds(t0, n), every, (depth + 4 - d) % 4]
-        else:
-            here = part(j, (row + 4 - d) % 4, every)
+        here = line(j, d, every)
         remote(here, here, y_send.at[j, d - 1], y_recv.at[j, d - 1], partner).wait_recv()
 
     def forward(j, up):
-        if up:
-            half = part(j, (row + 3) % 4, halves[0])
-            return remote(half, half, y_send.at[j, 1], y_recv.at[j, 1], at(1, 0))
-        half = part(j, (row + 1) % 4, halves[1])
-        return remote(half, half, y_send.at[j, 3], y_recv.at[j, 3], at(3, 0))
+        half, sem = (line(j, 1, halves[0]), 1) if up else (line(j, 3, halves[1]), 3)
+        return remote(half, half, y_send.at[j, sem], y_recv.at[j, sem], ahead(j, 1 if up else 3))
 
     def forward_wait(j, up):
-        half = part(j, (row + 2) % 4, halves[0 if up else 1])
-        sem = 1 if up else 3
+        half, sem = (line(j, 2, halves[0]), 1) if up else (line(j, 2, halves[1]), 3)
         remote(half, half, y_send.at[j, sem], y_recv.at[j, sem], partner).wait_recv()
 
     def c_copy(j, cycle):
-        t0, n, _ = CHUNKS[j]
+        t0, n = CHUNKS[j][:2]
         block = curr.at[cycle, pl.ds(t0, n)]
         return remote(block, block, c_send.at[j], c_recv.at[j], partner)
 
     def h_copy(j, up):
-        t0, n, _ = CHUNKS[j]
+        t0, n = CHUNKS[j][:2]
         if up:
             return remote(
                 edge_hi.at[pl.ds(t0, n)], halo_up.at[pl.ds(REACH + t0, n)], h_send.at[j, 0], h_recv.at[j, 0], (date, tile + 1)
@@ -208,12 +202,12 @@
     def onward(j):
         for d in (1, 3, 2):
             first_wait(j, d)
-        for d in (2, 1, 3) if CHUNKS[j][2] else (1, 3):
+        for d in (1, 3) if CHUNKS[j][3] else (2, 1, 3):
             second(j, d).start()
 
     def transpose(j):
-        t0, n, _ = CHUNKS[j]
-        if CHUNKS[j][2]:
+        t0, n = CHUNKS[j][:2]
+        if not CHUNKS[j][3]:
             for d in (1, 3, 2):
                 second_wait(j, d)
         else:
@@ -224,25 +218,27 @@
             curr[core, t] = gath[t].reshape(128, 128).T.reshape(16, 8, 128)
             return carry
 
-        lax.fori_loop(t0, t0 + n, turn, 0)
+        lax.fori_loop(t0, t0 + n, turn, 0, unroll=True)
         c_copy(j, core).start()
 
     def differences(j):
-        t0, n, _ = CHUNKS[j]
+        t0, n = CHUNKS[j][:2]
         loads[j].wait()
         c_copy(j, 1 - core).wait_recv()
 
         def one(t, carry):
-            for d in range(4):
-                sums = [None, None]
-                for p in range(16):
+            sums = {}
+            for p in range(16):
+                now = curr[0, t, p], curr[1, t, p]
+                for d in range(4):
                     past = arch[d, t, p]
                     for c in range(2):
-                        gap = curr[c, t, p] - past
+                        gap = now[c] - past
                         term = gap * gap * w_ref[p]
-                        sums[c] = term if p == 0 else sums[c] + term
+                        sums[c, d] = term if p == 0 else sums[c, d] + term
+            for d in range(4):
                 for c in range(2):
-                    v = sums[c]
+                    v = sums[c, d]
                     v = (
                         v
                         + jnp.where(lane > 0, pltpu.roll(v, 1, 1), 0.0)
@@ -267,7 +263,7 @@
     scored, sent, seen = set(), [0], set()
 
     def scores(j):
-        t0, n, _ = CHUNKS[j]
+        t0, n = CHUNKS[j][:2]
         if not seen:
             load_obs.wait()
 
@@ -317,7 +313,7 @@
             stop = ready[0] + 1
             while stop in ready:
                 stop += 1
-            lax.fori_loop(ready[0], stop, one, 0)
+            lax.fori_loop(ready[0], stop, one, 0, unroll=2)
             scored.update(range(ready[0], stop))
             ready = [t for t in ready if t >= stop]
         while sent[0] < BLOCKS and all(t in scored for t in range(sent[0] * BLOCK, (sent[0] + 1) * BLOCK)):
@@ -339,7 +335,7 @@
             pack[1, :, s, :] = (e0 * r0 + e1 * r1) / den
             return carry
 
-        lax.fori_loop(0, BLOCK, one, 0)
+        lax.fori_loop(0, BLOCK, one, 0, unroll=True)
         packed[b] = pack[...].reshape(128, 128).T.reshape(16, 8, 128)
         for o in range(15):
             r_copy(b, o).start()
@@ -396,9 +392,9 @@
     for j in range(len(CHUNKS)):
         for d in (1, 2, 3):
             first(j, d).wait_send()
-            if CHUNKS[j][2] or d != 2:
+            if d != 2 or not CHUNKS[j][3]:
                 second(j, d).wait_send()
-        if not CHUNKS[j][2]:
+        if CHUNKS[j][3]:
             forward(j, True).wait_send()
             forward(j, False).wait_send()
         c_copy(j, core).wait_send()

time: 52.5 us -> 49.8 us (0.949)
  Pallas kernels: 51 us -> 48.3 us
    pallas_call x1, Pallas kernels: 51 us -> 48.3 us  [local(): pl.pallas_call(kernel, out_shape=jax.ShapeDtypeStruct((2, 8, 4, LEADS), f...]
where the time goes in v3:
time: 49.8 us; the launch traced here: 49.7 us
  Pallas kernels  48.3 us (97%)
  local copies, waits for them, and re-layouts  1.38 us (3%)
    pallas_call x1, Pallas kernels, local(): pl.pallas_call(kernel, out_shape=jax.ShapeDtypeStruct((2, 8, 4, LEADS), f...  48.3 us
    unnamed x1, local copies, waits for them, and re-layouts  1.38 us

profile of v3, /device:TPU:7, one launch (start us, length us, event | category | flops | bytes accessed | tf_op | source)
XLA Modules:
  0.0 49.7 jit_solution(16868103280304991839)
XLA Ops:
  0.0 48.3 %shard_map.73 = f32[2,8,4,24]{3,2,1,0:T(4,128)} custom-call(f32[2,16,8,4,24]{4,3,2,1,0:T(4,128)} %bitcast.2, f32[4,24,16,8,128]{4,3,2,1,0:T(8,128)} %arch_hbm.1, f32[4,24,8,128]{3,2,1,0:T(8,128)} %obs_hbm.1, f32[16]{0:T(128)} %w_hbm.1, f32[24]{0:T(128)} %blur_hbm.1, s32[4]{0:T(128)} %cal_hbm.1, s32[2]{0:T(128)} %today_hbm.1), custom_call_target="tpu_custom_call" | custom-call | tf_op jit(solution)/shard_map/pallas_call | solution.py:424
  48.3 1.4 %copy.9 = f32[2,24,8,4]{1,3,2,0:T(4,128)} copy(f32[2,24,8,4]{1,3,2,0:T(4,128)} %bitcast.3) | data formatting | bytes 12288

commit v4 on v3

--- a/solution.py
+++ b/solution.py
@@ -11,7 +11,7 @@
 MESH = pl.DeviceIdType.MESH
 LEADS = 24
 REACH = 3
-CHUNKS = ((6, 6, False, True), (12, 6, False, True), (18, 6, False, True), (0, 6, True, False))
+CHUNKS = ((6, 7, False, True), (13, 7, False, True), (20, 4, False, True), (0, 6, True, False))
 STEPS = (
     ("F", 3), ("F", 0), ("F", 1), ("R", 0), ("F", 2), ("R", 1), ("T", 0), ("R", 2), ("T", 1), ("D", 0), ("T", 3), ("D", 1), ("T", 2), ("D", 3), ("S", 0), ("D", 2), ("S", 1), ("S", 3), ("S", 2),
 )

time: 49.8 us -> 49.7 us (level)
  no operation moved by 1% of the time
where the time goes in v4:
time: 49.7 us; the launch traced here: 49.5 us
  Pallas kernels  48.1 us (97%)
  local copies, waits for them, and re-layouts  1.38 us (3%)
    pallas_call x1, Pallas kernels, local(): pl.pallas_call(kernel, out_shape=jax.ShapeDtypeStruct((2, 8, 4, LEADS), f...  48.1 us
    unnamed x1, local copies, waits for them, and re-layouts  1.38 us

profile of v4, /device:TPU:7, one launch (start us, length us, event | category | flops | bytes accessed | tf_op | source)
XLA Modules:
  0.0 49.5 jit_solution(4846435012815903107)
XLA Ops:
  0.0 48.1 %shard_map.73 = f32[2,8,4,24]{3,2,1,0:T(4,128)} custom-call(f32[2,16,8,4,24]{4,3,2,1,0:T(4,128)} %bitcast.2, f32[4,24,16,8,128]{4,3,2,1,0:T(8,128)} %arch_hbm.1, f32[4,24,8,128]{3,2,1,0:T(8,128)} %obs_hbm.1, f32[16]{0:T(128)} %w_hbm.1, f32[24]{0:T(128)} %blur_hbm.1, s32[4]{0:T(128)} %cal_hbm.1, s32[2]{0:T(128)} %today_hbm.1), custom_call_target="tpu_custom_call" | custom-call | tf_op jit(solution)/shard_map/pallas_call | solution.py:424
  48.2 1.4 %copy.9 = f32[2,24,8,4]{1,3,2,0:T(4,128)} copy(f32[2,24,8,4]{1,3,2,0:T(4,128)} %bitcast.3) | data formatting | bytes 12288

commit v5 on v4

--- a/solution.py
+++ b/solution.py
@@ -13,7 +13,7 @@
 REACH = 3
 CHUNKS = ((6, 7, False, True), (13, 7, False, True), (20, 4, False, True), (0, 6, True, False))
 STEPS = (
-    ("F", 3), ("F", 0), ("F", 1), ("R", 0), ("F", 2), ("R", 1), ("T", 0), ("R", 2), ("T", 1), ("D", 0), ("T", 3), ("D", 1), ("T", 2), ("D", 3), ("S", 0), ("D", 2), ("S", 1), ("S", 3), ("S", 2),
+    ("F", 3), ("F", 0), ("F", 1), ("R", 0), ("F", 2), ("R", 1), ("T", 0), ("R", 2), ("T", 1), ("D", 0), ("T", 3), ("D", 1), ("T", 2), ("D", 3), ("D", 2), ("S", 0), ("S", 1), ("S", 3), ("S", 2),
 )
 BLOCK = 8
 BLOCKS = LEADS // BLOCK

time: 49.7 us -> 49.4 us (level); the launches traced: 49.5 us -> 48.5 us
  Pallas kernels: 48.1 us -> 47.1 us
    pallas_call x1, Pallas kernels: 48.1 us -> 47.1 us  [local(): pl.pallas_call(kernel, out_shape=jax.ShapeDtypeStruct((2, 8, 4, LEADS), f...]
where the time goes in v5:
time: 49.4 us; the launch traced here: 48.5 us
  Pallas kernels  47.1 us (95%)
  local copies, waits for them, and re-layouts  1.38 us (3%)
    pallas_call x1, Pallas kernels, local(): pl.pallas_call(kernel, out_shape=jax.ShapeDtypeStruct((2, 8, 4, LEADS), f...  47.1 us
    unnamed x1, local copies, waits for them, and re-layouts  1.38 us

profile of v5, /device:TPU:7, one launch (start us, length us, event | category | flops | bytes accessed | tf_op | source)
XLA Modules:
  0.0 48.5 jit_solution(639222193296754982)
XLA Ops:
  0.0 47.1 %shard_map.73 = f32[2,8,4,24]{3,2,1,0:T(4,128)} custom-call(f32[2,16,8,4,24]{4,3,2,1,0:T(4,128)} %bitcast.2, f32[4,24,16,8,128]{4,3,2,1,0:T(8,128)} %arch_hbm.1, f32[4,24,8,128]{3,2,1,0:T(8,128)} %obs_hbm.1, f32[16]{0:T(128)} %w_hbm.1, f32[24]{0:T(128)} %blur_hbm.1, s32[4]{0:T(128)} %cal_hbm.1, s32[2]{0:T(128)} %today_hbm.1), custom_call_target="tpu_custom_call" | custom-call | tf_op jit(solution)/shard_map/pallas_call | solution.py:424
  47.1 1.4 %copy.9 = f32[2,24,8,4]{1,3,2,0:T(4,128)} copy(f32[2,24,8,4]{1,3,2,0:T(4,128)} %bitcast.3) | data formatting | bytes 12288
